TPU v7x, 32 devices: a whole 2x2x4 slice. The times are simulated.
32 devices in a mesh: seq: 8 (over y, x, core), tensor: 4 (over z).
Axes of the slice: x: 2, y: 2, z: 4, core: 2. Of those that a mesh axis runs over, the one named last changes fastest.
Arguments:
- inputs: bfloat16 [32768, 2048], P('seq', 'tensor'), may hold values from -6 to 6
- out_grad: bfloat16 [32768, 2048], P('seq', 'tensor'), may hold values from -6 to 6
- router_score: float32 [32768], P('seq'), may hold values from 0.1 to 1
- route_index: int32 [8, 512], P('seq'), may hold values from 0 to 4095, as said below
- block_count: int32 [8], P('seq'), may hold values from 1 to 4, 16 in all
- w_in: bfloat16 [2048, 8192], P('seq', 'tensor'), may hold values from -0.125 to 0.125
- w_out: bfloat16 [8192, 2048], P('tensor', 'seq'), may hold values from -0.0625 to 0.0625
Outputs:
- input_grad: bfloat16 [32768, 2048], P('seq', 'tensor')
- score_grad: float32 [32768], P('seq')
Inputs may be any that keep to these rules, and one draw needn't show every extreme that they name: `route_index`: row j holds 512 distinct positions within shard j; its first block_count[j] * 128 entries are the routed tokens, the rest padding. `block_count`: the counts sum to exactly 16.
All inputs are finite; a program needn't handle non-finite values.
Results may differ from a plain program's by a relative error of at most 0.012.
Values may be sent and summed in bfloat16 or wider, within the bound.
A program may use at most 128 MiB of HBM per device.

v0:
```python
import jax
import jax.numpy as jnp
from jax import lax
from jax.sharding import PartitionSpec as P

BLK = 128


gelu_coeff = 0.7978845608028654
cubic_coeff = 0.044715


def gelu_pair(values):
    inner = gelu_coeff * (values + cubic_coeff * values * values * values)
    tangent = jnp.tanh(inner)
    forward = 0.5 * values * (1.0 + tangent)
    slope = 0.5 * (1.0 + tangent) + 0.5 * values * (1.0 - tangent * tangent) * gelu_coeff * (
        1.0 + 3.0 * cubic_coeff * values * values
    )
    return (forward, slope)


def heavy_backward(chosen, grads, scores, w_in, w_out):
    full_inputs, full_grads = (
        lax.all_gather(chosen, "tensor", axis=1, tiled=True),
        lax.all_gather(grads, "tensor", axis=1, tiled=True),
    )
    weight_rows = lax.all_gather(w_in, "seq", axis=0, tiled=True)
    hidden = jnp.dot(full_inputs, weight_rows, preferred_element_type=jnp.float32)
    upstream = lax.dot_general(
        full_grads,
        lax.all_gather(w_out, "seq", axis=1, tiled=True),
        (((1,), (1,)), ((), ())),
        preferred_element_type=jnp.float32,
    )
    forward, slope = gelu_pair(hidden)
    active = forward.astype(jnp.bfloat16)
    score_part = jnp.sum(upstream * active.astype(jnp.float32), axis=1)
    row_scores = lax.psum(score_part, "tensor")
    hidden_grad = (scores[:, None] * upstream * slope).astype(jnp.bfloat16)
    input_part = lax.dot_general(
        hidden_grad, weight_rows, (((1,), (1,)), ((), ())), preferred_element_type=jnp.float32
    )
    row_grads = lax.psum_scatter(
        input_part.astype(jnp.bfloat16), "tensor", scatter_dimension=1, tiled=True
    )
    return (row_grads, row_scores)


def per_device(inputs, out_grad, router_score, route_index, block_count, w_in, w_out):
    route_rows = route_index.shape[1]
    picked = route_index[0]
    own_count = block_count[0]
    sel_inputs = jnp.take(inputs, picked, axis=0)
    sel_grads = jnp.take(out_grad, picked, axis=0)
    sel_score = jnp.take(router_score, picked, axis=0)
    slot_ids = jnp.arange(route_rows, dtype=jnp.int32)
    mine_grads, mine_scores = heavy_backward(sel_inputs, sel_grads, sel_score, w_in, w_out)
    is_mine = slot_ids < own_count * BLK
    mine_grads = jnp.where(is_mine[:, None], mine_grads, jnp.zeros((), jnp.bfloat16))
    mine_scores = jnp.where(is_mine, mine_scores, 0.0)
    input_grad = jnp.zeros(inputs.shape, jnp.bfloat16).at[picked].set(mine_grads)
    score_grad = jnp.zeros(router_score.shape, jnp.float32).at[picked].set(mine_scores)
    return (input_grad, score_grad)


def solution(mesh):
    placed = (
        P("seq", "tensor"),
        P("seq", "tensor"),
        P("seq"),
        P("seq", None),
        P("seq"),
        P("seq", "tensor"),
        P("tensor", "seq"),
    )
    return jax.shard_map(
        per_device,
        mesh=mesh,
        in_specs=placed,
        out_specs=(P("seq", "tensor"), P("seq")),
        check_vma=False,
    )
```

profile of v0, /device:TPU:0, one launch (start us, length us, event | category | flops | bytes accessed | tf_op | source)
XLA Modules:
  0.0 308.7 jit_solution(1608539325587748638)
XLA Ops:
  7.2 0.0 copy-start
  7.2 0.0 all-gather.9.cloned.1.call-start
  7.2 0.7 compare_select_fusion
  7.9 0.7 compare_select_fusion.1
  8.6 0.0 copy-done
  8.6 3.1 %gather_fusion = f32[512]{0:T(512)S(1)} fusion(f32[4096]{0:T(1024)S(1)} %copy-done, s32[1024]{0:T(1024)S(1)} %pad_clamp_fusion.1), kind=kCustom, calls=%fused_computation.2 | custom fusion | bytes 6144 | tf_op jit(solution)/shard_map/jit(_take)/gather | solution.py:56
  11.8 0.7 broadcast_select_fusion.3
  12.5 4.7 %gather_fusion.1 = bf16[512,512]{1,0:T(8,128)(2,1)S(1)} fusion(bf16[4096,512]{1,0:T(8,128)(2,1)} %param.10, s32[1024]{0:T(1024)S(1)} %pad_clamp_fusion), kind=kCustom, calls=%fused_computation.clone | custom fusion | bytes 1050624 | tf_op jit(solution)/shard_map/jit(_take)/gather | solution.py:55
  17.2 4.7 %gather_fusion.2 = bf16[512,512]{1,0:T(8,128)(2,1)S(1)} fusion(bf16[4096,512]{1,0:T(8,128)(2,1)} %param.9, s32[1024]{0:T(1024)S(1)} %pad_clamp_fusion), kind=kCustom, calls=%fused_computation.1.clone | custom fusion | bytes 1050624 | tf_op jit(solution)/shard_map/jit(_take)/gather | solution.py:54
  21.9 1.1 broadcast_select_fusion.1
  23.0 0.0 all-gather.9.cloned.1.call-update
  23.1 0.0 all-gather.11.cloned.1.call-start
  23.1 0.7 all-gather.11.cloned.1.call-update
  23.8 0.0 all-gather.5.cloned.1.call-start
  23.9 0.7 all-gather.5.cloned.1.call-update
  24.5 0.0 all-gather.7.cloned.1.call-start
  24.6 0.5 all-gather.7.cloned.1.call-update
  25.1 0.2 reduce-scatter.2.cloned.1.call-start
  25.3 46.5 %all-gather.9.cloned.1.call-done = bf16[512,2048]{1,0:T(8,128)(2,1)} async-done(((bf16[512,512]{1,0:T(8,128)(2,1)}), bf16[512,2048]{1,0:T(8,128)(2,1)}) %all-gather.9.cloned.1.call-update) | async-done | bytes 2097168 | tf_op jit(solution)/shard_map/all_gather | solution.py:25
  71.8 55.0 %all-gather.11.cloned.1.call-done = bf16[2048,2048]{1,0:T(8,128)(2,1)} async-done(((bf16[256,2048]{1,0:T(8,128)(2,1)}), bf16[2048,2048]{1,0:T(8,128)(2,1)}) %all-gather.11.cloned.1.call-update) | async-done | bytes 8388624 | tf_op jit(solution)/shard_map/all_gather | solution.py:28
  126.9 10.5 %fusion.25 = f32[512,2048]{1,0:T(8,128)} fusion(bf16[512,2048]{1,0:T(8,128)(2,1)} %all-gather.9.cloned.1.call-done, bf16[2048,2048]{1,0:T(8,128)(2,1)} %all-gather.11.cloned.1.call-done), kind=kOutput, calls=%fused_computation.44 | convolution fusion | flops 4294967296 | bytes 14680064 | tf_op jit(solution)/shard_map/dot_general | solution.py:29
  137.4 37.0 %all-gather.5.cloned.1.call-done = bf16[512,2048]{1,0:T(8,128)(2,1)} async-done(((bf16[512,512]{1,0:T(8,128)(2,1)}), bf16[512,2048]{1,0:T(8,128)(2,1)}) %all-gather.5.cloned.1.call-update) | async-done | bytes 2097168 | tf_op jit(solution)/shard_map/all_gather | solution.py:26
  174.4 56.4 %all-gather.7.cloned.1.call-done = bf16[2048,2048]{1,0:T(8,128)(2,1)} async-done(((bf16[2048,256]{1,0:T(8,128)(2,1)}), bf16[2048,2048]{1,0:T(8,128)(2,1)}) %all-gather.7.cloned.1.call-update) | async-done | bytes 8388624 | tf_op jit(solution)/shard_map/all_gather | solution.py:32
  230.9 0.0 copy-start.1
  230.9 0.0 copy-start.2
  230.9 12.1 %multiply_reduce_fusion = (f32[512]{0:T(512)S(1)}, f32[512,2048]{1,0:T(8,128)}) fusion(f32[512,2048]{1,0:T(8,128)} %fusion.25, bf16[512,2048]{1,0:T(8,128)(2,1)} %all-gather.5.cloned.1.call-done, bf16[2048,2048]{1,0:T(8,128)(2,1)} %all-gather.7.cloned.1.call-done), kind=kOutput, calls=%fused_computation.14 | convolution fusion | flops 4307549696 | bytes 18876416 | tf_op jit(solution)/shard_map/dot_general | solution.py:30
  242.9 0.0 copy-done.1
  243.0 0.0 copy-done.2
  243.0 9.3 %convolution_convert_fusion = bf16[512,2048]{1,0:T(8,128)(2,1)} fusion(bf16[2048,2048]{1,0:T(8,128)(2,1)S(1)} %copy-done.1, f32[512,2048]{1,0:T(8,128)S(1)} %copy-done.2, f32[512,2048]{1,0:T(8,128)} %get-tuple-element.8, f32[512]{0:T(512)S(1)} %get-tuple-element.3), kind=kOutput, calls=%fused_computation.16 | convolution fusion | flops 4316987392 | bytes 18876416 | tf_op jit(solution)/shard_map/dot_general | solution.py:41
  252.3 0.0 reduce-scatter.2.cloned.1.call-update
  253.0 11.9 %psum.7 = f32[512]{0:T(512)S(1)} all-reduce(f32[512]{0:T(512)S(1)} %get-tuple-element.7), channel_id=1, replica_groups=mesh['seq'=8,'tensor'=4] {'tensor'}, use_global_device_ids=true, to_apply=%region_3.5 | all-reduce | flops 512 | bytes 4096 | tf_op jit(solution)/shard_map/psum | solution.py:39
  264.9 3.0 scatter_custom_fusion.1
  267.9 28.5 %reduce-scatter.2.cloned.1.call-done = bf16[512,512]{1,0:T(8,128)(2,1)} async-done(((bf16[512,2048]{1,0:T(8,128)(2,1)}), bf16[512,512]{1,0:T(8,128)(2,1)}) %reduce-scatter.2.cloned.1.call-update) | async-done | bytes 524304 | tf_op jit(solution)/shard_map/reduce_scatter | solution.py:44
  296.4 5.8 %scatter_custom_fusion = bf16[4096,512]{1,0:T(8,128)(2,1)} fusion(s32[512]{0:T(512)S(1)} %bitcast.14, bf16[]{:T(256)} %constant.7.clone.1, bf16[512,512]{1,0:T(8,128)(2,1)} %reduce-scatter.2.cloned.1.call-done, pred[512]{0:T(512)(128)(4,1)S(1)} %iota_compare_fusion), kind=kCustom, calls=%fused_computation.22 | custom fusion | flops 262144 | bytes 4720128 | tf_op jit(solution)/shard_map/scatter | solution.py:62
  (4 shorter events, 0.0 us)
Async XLA Ops:
  7.2 1.4 copy-start
  7.2 64.7 %all-gather.9.cloned.1.call-start = ((), (), s32[]{:S(2)}) async-start(), calls=%async_computation.3 | async-start | bytes 2621440 | tf_op jit(solution)/shard_map/all_gather | solution.py:25
  23.1 103.8 %all-gather.11.cloned.1.call-start = ((), (), s32[]{:S(2)}) async-start(), calls=%async_computation.4 | async-start | bytes 9437184 | tf_op jit(solution)/shard_map/all_gather | solution.py:28
  23.8 150.6 %all-gather.5.cloned.1.call-start = ((), (), s32[]{:S(2)}) async-start(), calls=%async_computation.1 | async-start | bytes 2621440 | tf_op jit(solution)/shard_map/all_gather | solution.py:26
  24.5 206.3 %all-gather.7.cloned.1.call-start = ((), (), s32[]{:S(2)}) async-start(), calls=%async_computation.2 | async-start | bytes 9437184 | tf_op jit(solution)/shard_map/all_gather | solution.py:32
  25.1 271.3 %reduce-scatter.2.cloned.1.call-start = ((), (), s32[]{:S(2)}) async-start(), calls=%async_computation.5 | async-start | bytes 2621440 | tf_op jit(solution)/shard_map/reduce_scatter | solution.py:44
  230.9 12.1 %copy-start.1 = (bf16[2048,2048]{1,0:T(8,128)(2,1)S(1)}, bf16[2048,2048]{1,0:T(8,128)(2,1)}, u32[]{:S(2)}) copy-start(bf16[2048,2048]{1,0:T(8,128)(2,1)} %all-gather.11.cloned.1.call-done) | copy-start | bytes 25165828
  230.9 12.1 %copy-start.2 = (f32[512,2048]{1,0:T(8,128)S(1)}, f32[512,2048]{1,0:T(8,128)}, u32[]{:S(2)}) copy-start(f32[512,2048]{1,0:T(8,128)} %fusion.25) | copy-start | bytes 12582916
Sparse Core Ops, SparseCore 0:
  23.2 48.6 all-gather.8
  73.7 53.0 all-gather.10
  128.4 45.9 all-gather.4
  176.2 54.6 all-gather.6
  252.4 43.9 reduce-scatter.1
where the time goes:
time: 309 us
  waiting for transfers between devices  225 us (73%)
  matrix products  31.9 us (10%)
  local copies, waits for them, and re-layouts  15.6 us (5%)
  between operations  14.5 us (5%)
  blocking collectives  11.9 us (4%)
  other arithmetic  9.01 us (3%)
    all_gather x1, waiting for transfers between devices, heavy_backward(): lax.all_gather(w_out, 'seq', axis=1, tiled=True)  56.4 us
    all_gather x1, waiting for transfers between devices, heavy_backward(): weight_rows = lax.all_gather(w_in, 'seq', axis=0, tiled=True)  55 us
    all_gather x1, waiting for transfers between devices, heavy_backward(): lax.all_gather(chosen, 'tensor', axis=1, tiled=True)  46.5 us
    all_gather x1, waiting for transfers between devices, heavy_backward(): lax.all_gather(grads, 'tensor', axis=1, tiled=True)  37 us
    reduce_scatter x1, waiting for transfers between devices, heavy_backward(): lax.psum_scatter(input_part.astype(jnp.bfloat16), 'tensor', scatter_dimen...  28.5 us
    dot_general x1, matrix products, heavy_backward(): lax.dot_general(full_grads, lax.all_gather(w_out, 'seq', axis=1, tiled=Tr...  12.1 us
    psum x1, blocking collectives, heavy_backward(): row_scores = lax.psum(score_part, 'tensor')  11.9 us
    dot_general x1, matrix products, heavy_backward(): jnp.dot(full_inputs, weight_rows, preferred_element_type=jnp.float32)  10.5 us
  transfers between devices with their start and end apart: 5, of which 5 were waited for; matrix products, arithmetic and copies ran while one was open for 4% of the time, Pallas kernels for 0%

commit v1 on v0

v1 whole, which is shorter than its diff:
```python
import functools

import jax
import jax.numpy as jnp
from jax import lax
from jax.experimental import pallas as pl
from jax.experimental.pallas import tpu as pltpu
from jax.sharding import PartitionSpec as P

BLK = 128
MESH = pl.DeviceIdType.MESH
F32, BF16 = jnp.float32, jnp.bfloat16
NT = (((1,), (1,)), ((), ()))
NN = (((1,), (0,)), ((), ()))

gelu_coeff = 0.7978845608028654
cubic_coeff = 0.044715


def gelu_pair(values):
    square = values * values
    tangent = jnp.tanh(gelu_coeff * (values + cubic_coeff * square * values))
    half = 0.5 * (1.0 + tangent)
    slope = half + 0.5 * values * (1.0 - tangent * tangent) * gelu_coeff * (
        1.0 + 3.0 * cubic_coeff * square
    )
    return values * half, slope


def dot(a, b, dims):
    return lax.dot_general(a, b, dims, preferred_element_type=F32)


def heavy_kernel(
    n, nt, idx_ref, inputs_ref, grads_ref, win_ref, wout_ref, rows_ref, score_ref,
    tok_buf, x_buf, g_buf, win_buf, wout_buf, act_buf, slope_buf, hg_buf,
    pair_send, pair_recv, z_send, z_recv, own_buf, sc_out, sc_pair, sc_z,
    tok_sem, wl_sem, w_send, w_recv, z_ssem, z_rsem, p_ssem, p_rsem,
    os_sem, or_sem, oz_ssem, oz_rsem, ss_sem, sr_sem,
):
    s, t = lax.axis_index("seq"), lax.axis_index("tensor")
    c, k = lax.div(s, 2), lax.rem(s, 2)
    chips = n // 2
    toks, width = inputs_ref.shape
    rows = idx_ref.shape[1]
    depth = win_ref.shape[0]
    half = win_ref.shape[1] // 2
    other = 1 - k
    partner = c * 2 + other
    square = chips == 4

    if square:
        out_chip = [c + 1 - 2 * lax.rem(c, 2), lax.rem(c + 2, 4), 3 - c]
        in_chip = out_chip
    else:
        out_chip = [lax.rem(c + r, chips) for r in range(1, chips)]
        in_chip = [lax.rem(c + chips - r, chips) for r in range(1, chips)]

    def t_out(r):
        return lax.rem(t + r, nt)

    def t_in(r):
        return lax.rem(t + nt - r, nt)

    load = [
        pltpu.make_async_copy(src, tok_buf.at[i], tok_sem.at[i])
        for i, src in enumerate((inputs_ref, grads_ref))
    ]
    for cp in load:
        cp.start()

    def weight_src(w, core):
        start = pl.multiple_of(core * half, half)
        if w == 0:
            return win_ref.at[:, pl.ds(start, half)]
        return wout_ref.at[pl.ds(start, half), :]

    def weight_dst(w, owner):
        if w == 0:
            return win_buf.at[pl.ds(pl.multiple_of(owner * depth, depth), depth), :]
        return wout_buf.at[owner]

    local = [
        pltpu.make_async_copy(weight_src(w, k), weight_dst(w, s), wl_sem.at[w]) for w in range(2)
    ]
    for cp in local:
        cp.start()

    barrier = pltpu.get_barrier_semaphore()
    for chip in out_chip:
        for core in range(2):
            pl.semaphore_signal(
                barrier, inc=1, device_id={"seq": chip * 2 + core}, device_id_type=MESH
            )
    pl.semaphore_signal(barrier, inc=1, device_id={"seq": partner}, device_id_type=MESH)
    for r in range(1, nt):
        pl.semaphore_signal(barrier, inc=1, device_id={"tensor": t_out(r)}, device_id_type=MESH)
    pl.semaphore_wait(barrier, 2 * (chips - 1) + 1 + nt - 1)

    def weight_copy(w, r, q):
        core = k if q == 0 else other
        return pltpu.make_async_remote_copy(
            src_ref=weight_src(w, core), dst_ref=weight_dst(w, s),
            send_sem=w_send.at[w, r, q], recv_sem=w_recv.at[w, r, q],
            device_id={"seq": out_chip[r] * 2 + core}, device_id_type=MESH,
        )

    def weight_hop(w, q):
        came, go = (0, 1) if q == 0 else (1, 0)
        owner = in_chip[came] * 2 + (k if q == 0 else other)
        return pltpu.make_async_remote_copy(
            src_ref=weight_dst(w, owner), dst_ref=weight_dst(w, owner),
            send_sem=w_send.at[w, 2, q], recv_sem=w_recv.at[w, 2, q],
            device_id={"seq": out_chip[go] * 2 + k}, device_id_type=MESH,
        )

    def weight_landed(w, r, q):
        owner = in_chip[r] * 2 + (k if q == 0 else other)
        return pltpu.make_async_remote_copy(
            src_ref=weight_dst(w, owner), dst_ref=weight_dst(w, owner),
            send_sem=w_send.at[w, r, q], recv_sem=w_recv.at[w, r, q],
            device_id={"seq": owner}, device_id_type=MESH,
        )

    def weight_pair(w, owner):
        return pltpu.make_async_remote_copy(
            src_ref=weight_src(w, other), dst_ref=weight_dst(w, owner),
            send_sem=w_send.at[w, chips - 1, 0], recv_sem=w_recv.at[w, chips - 1, 0],
            device_id={"seq": partner}, device_id_type=MESH,
        )

    direct = range(2) if square else range(chips - 1)

    def start_weights(w):
        for q in range(2):
            for r in direct:
                weight_copy(w, r, q).start()
        weight_pair(w, s).start()

    def pass_weights(w):
        if square:
            for q in range(2):
                weight_landed(w, q, q).wait_recv()
                weight_hop(w, q).start()

    def finish_weights(w):
        local[w].wait()
        weight_pair(w, partner).wait_recv()
        for r in range(chips - 1):
            for q in range(2):
                if square and r == q:
                    continue
                weight_landed(w, r, q).wait_recv()

    def drain_weights(w):
        weight_pair(w, s).wait_send()
        for q in range(2):
            for r in direct:
                weight_copy(w, r, q).wait_send()
            if square:
                weight_hop(w, q).wait_send()

    tokens = (x_buf, g_buf)

    def piece(v, shard, column):
        return tokens[v].at[shard, :, pl.ds(pl.multiple_of(column * width, width), width)]

    def gather(v):
        load[v].wait()
        step = min(512, toks)
        column = jnp.transpose(jnp.broadcast_to(idx_ref[...], (128, rows)))[:, :1]
        dst = piece(v, k, t)
        total = jnp.zeros((rows, width), F32)
        x_own = own_buf

        x_own[...] = total

        def body(i, carry):
            start = pl.multiple_of(i * step, step)
            spots = lax.broadcasted_iota(jnp.int32, (rows, step), 1) + i * step
            hot = jnp.where(column == spots, 1.0, 0.0).astype(BF16)
            x_own[...] += dot(hot, tok_buf[v, pl.ds(start, step), :], NN)
            return carry

        lax.fori_loop(0, toks // step, body, 0)
        dst[...] = x_own[...].astype(BF16)

    def z_copy(v, r):
        return pltpu.make_async_remote_copy(
            src_ref=piece(v, k, t), dst_ref=piece(v, k, t),
            send_sem=z_ssem.at[v, r], recv_sem=z_rsem.at[v, r],
            device_id={"tensor": t_out(r)}, device_id_type=MESH,
        )

    def z_landed(v, r):
        return pltpu.make_async_remote_copy(
            src_ref=piece(v, k, t_in(r)), dst_ref=piece(v, k, t_in(r)),
            send_sem=z_ssem.at[v, r], recv_sem=z_rsem.at[v, r],
            device_id={"tensor": t_in(r)}, device_id_type=MESH,
        )

    def pair_copy(v, r, shard):
        return pltpu.make_async_remote_copy(
            src_ref=piece(v, shard, t_in(r)), dst_ref=piece(v, shard, t_in(r)),
            send_sem=p_ssem.at[v, r], recv_sem=p_rsem.at[v, r],
            device_id={"seq": partner}, device_id_type=MESH,
        )

    def start_tokens(v):
        for r in range(1, nt):
            z_copy(v, r).start()
        pair_copy(v, 0, k).start()

    def pass_tokens(v):
        for r in range(1, nt):
            z_landed(v, r).wait_recv()
            pair_copy(v, r, k).start()

    def finish_tokens(v):
        for r in range(nt):
            pair_copy(v, r, other).wait_recv()

    def drain_tokens(v):
        for r in range(1, nt):
            z_copy(v, r).wait_send()
        for r in range(nt):
            pair_copy(v, r, k).wait_send()

    start_weights(0)
    gather(0)
    start_tokens(0)
    gather(1)
    pass_weights(0)
    start_weights(1)
    pass_tokens(0)
    start_tokens(1)
    finish_weights(0)
    finish_tokens(0)

    ft = min(256, half)

    def hidden_step(i, carry):
        shard, f = lax.div(i, half // ft), lax.rem(i, half // ft)
        cols = pl.ds(pl.multiple_of(f * ft, ft), ft)
        hidden = dot(x_buf[shard], win_buf[:, cols], NN)
        forward, slope = gelu_pair(hidden)
        act_buf[shard, :, cols] = forward.astype(BF16)
        slope_buf[shard, :, cols] = slope
        return carry

    lax.fori_loop(0, 2 * (half // ft), hidden_step, 0)

    pass_weights(1)
    pass_tokens(1)
    finish_weights(1)
    finish_tokens(1)

    def upstream(shard):
        sc_out[...] = jnp.zeros_like(sc_out)

        def step(f, carry):
            cols = pl.ds(pl.multiple_of(f * ft, ft), ft)
            weights = jnp.concatenate([wout_buf[i, cols, :] for i in range(n)], axis=1)
            up = dot(g_buf[shard], weights, NT)
            hg_buf[:, cols] = (up * slope_buf[shard, :, cols]).astype(BF16)
            terms = up * act_buf[shard, :, cols].astype(F32)
            part = terms[:, :128]
            for i in range(1, ft // 128):
                part = part + terms[:, i * 128:(i + 1) * 128]
            sc_out[...] += part
            return carry

        lax.fori_loop(0, half // ft, step, 0)
        line = jnp.sum(jnp.transpose(sc_out[...]), axis=0, keepdims=True)
        return jnp.broadcast_to(line, (8, rows))

    def grads_of(column):
        span = pl.ds(pl.multiple_of(column * width, width), width)
        return dot(hg_buf[...], win_buf[span, :], NT)

    def o_pair(r):
        return pltpu.make_async_remote_copy(
            src_ref=pair_send.at[r], dst_ref=pair_recv.at[r],
            send_sem=os_sem.at[r], recv_sem=or_sem.at[r],
            device_id={"seq": partner}, device_id_type=MESH,
        )

    def o_z(r):
        return pltpu.make_async_remote_copy(
            src_ref=z_send.at[r - 1], dst_ref=z_recv.at[r - 1],
            send_sem=oz_ssem.at[r], recv_sem=oz_rsem.at[r],
            device_id={"tensor": t_out(r)}, device_id_type=MESH,
        )

    def s_pair():
        return pltpu.make_async_remote_copy(
            src_ref=sc_pair.at[0], dst_ref=sc_pair.at[1],
            send_sem=ss_sem.at[0], recv_sem=sr_sem.at[0],
            device_id={"seq": partner}, device_id_type=MESH,
        )

    def s_z(r):
        return pltpu.make_async_remote_copy(
            src_ref=sc_z.at[0], dst_ref=sc_z.at[r],
            send_sem=ss_sem.at[r], recv_sem=sr_sem.at[r],
            device_id={"tensor": t_out(r)}, device_id_type=MESH,
        )

    order = list(range(1, nt)) + [0]
    sc_pair[0] = upstream(other)
    s_pair().start()
    for r in order:
        pair_send[r] = grads_of(t_out(r)).astype(BF16)
        o_pair(r).start()

    mine = upstream(k)
    s_pair().wait_recv()
    sc_z[0] = mine + sc_pair[1]
    for r in range(1, nt):
        s_z(r).start()
    for r in order:
        part = grads_of(t_out(r))
        o_pair(r).wait_recv()
        part = part + pair_recv[r].astype(F32)
        if r == 0:
            own_buf[...] = part
        else:
            z_send[r - 1] = part.astype(BF16)
            o_z(r).start()

    drain_weights(0)
    drain_weights(1)
    drain_tokens(0)
    drain_tokens(1)
    s_pair().wait_send()
    for r in range(nt):
        o_pair(r).wait_send()
    for r in range(1, nt):
        s_z(r).wait()
    total = sc_z[0]
    for r in range(1, nt):
        total = total + sc_z[r]
    score_ref[...] = total
    for r in range(1, nt):
        o_z(r).wait()
    full = own_buf[...]
    for r in range(1, nt):
        full = full + z_recv[r - 1].astype(F32)
    rows_ref[...] = full.astype(BF16)


def scatter_kernel(count_ref, idx_ref, rows_ref, line_ref, score_ref, grad_ref, out_ref):
    tile = grad_ref.shape[0]
    slots = idx_ref.shape[1]
    live = lax.broadcasted_iota(jnp.int32, (1, slots), 1) < count_ref[0] * BLK
    picked = jnp.where(live, idx_ref[...], -1)
    spots = lax.broadcasted_iota(jnp.int32, (tile, slots), 0) + pl.program_id(0) * tile
    hot = jnp.where(spots == picked, 1.0, 0.0).astype(BF16)
    scale = jnp.transpose(jnp.broadcast_to(score_ref[...], (128, tile)))[:, :1]
    grad_ref[...] = (dot(hot, rows_ref[...], NN) * scale).astype(BF16)
    rest = jnp.broadcast_to(line_ref[:1, :], (16, slots))
    total = jnp.zeros((16, tile), F32)
    for _ in range(3):
        head = rest.astype(BF16)
        total = total + dot(head, hot, NT)
        rest = rest - head.astype(F32)
    out_ref[...] = total[:1, :]


def per_device(n, nt, inputs, out_grad, router_score, route_index, block_count, w_in, w_out):
    toks, width = inputs.shape
    rows = route_index.shape[1]
    depth, ff = w_in.shape
    half = ff // 2
    dim = width * nt
    chips = n // 2
    dma = pltpu.SemaphoreType.DMA
    vm = pl.BlockSpec(memory_space=pltpu.VMEM)
    hbm = pl.BlockSpec(memory_space=pl.ANY)
    row_grads, lines = pl.pallas_call(
        functools.partial(heavy_kernel, n, nt),
        out_shape=(
            jax.ShapeDtypeStruct((rows, width), BF16),
            jax.ShapeDtypeStruct((8, rows), F32),
        ),
        in_specs=[vm, hbm, hbm, hbm, hbm],
        out_specs=(vm, vm),
        scratch_shapes=[
            pltpu.VMEM((2, toks, width), BF16),
            pltpu.VMEM((2, rows, dim), BF16),
            pltpu.VMEM((2, rows, dim), BF16),
            pltpu.VMEM((n * depth, half), BF16),
            pltpu.VMEM((n, half, depth), BF16),
            pltpu.VMEM((2, rows, half), BF16),
            pltpu.VMEM((2, rows, half), F32),
            pltpu.VMEM((rows, half), BF16),
            pltpu.VMEM((nt, rows, width), BF16),
            pltpu.VMEM((nt, rows, width), BF16),
            pltpu.VMEM((nt - 1, rows, width), BF16),
            pltpu.VMEM((nt - 1, rows, width), BF16),
            pltpu.VMEM((rows, width), F32),
            pltpu.VMEM((rows, 128), F32),
            pltpu.VMEM((2, 8, rows), F32),
            pltpu.VMEM((nt, 8, rows), F32),
            dma((2,)), dma((2,)),
            dma((2, chips, 2)), dma((2, chips, 2)),
            dma((2, nt)), dma((2, nt)),
            dma((2, nt)), dma((2, nt)),
            dma((nt,)), dma((nt,)),
            dma((nt,)), dma((nt,)),
            dma((nt,)), dma((nt,)),
        ],
        compiler_params=pltpu.CompilerParams(
            collective_id=0, has_side_effects=True, vmem_limit_bytes=58 * 2**20
        ),
        name="heavy",
    )(route_index, inputs, out_grad, w_in, w_out)

    tile = min(1024, toks)
    input_grad, score_grad = pl.pallas_call(
        scatter_kernel,
        grid=(toks // tile,),
        out_shape=(
            jax.ShapeDtypeStruct((toks, width), BF16),
            jax.ShapeDtypeStruct((1, toks), F32),
        ),
        in_specs=[
            pl.BlockSpec(memory_space=pltpu.SMEM),
            pl.BlockSpec((1, rows), lambda i: (0, 0)),
            pl.BlockSpec((rows, width), lambda i: (0, 0)),
            pl.BlockSpec((8, rows), lambda i: (0, 0)),
            pl.BlockSpec((1, tile), lambda i: (0, i)),
        ],
        out_specs=(
            pl.BlockSpec((tile, width), lambda i: (i, 0)),
            pl.BlockSpec((1, tile), lambda i: (0, i)),
        ),
        compiler_params=pltpu.CompilerParams(vmem_limit_bytes=32 * 2**20),
        name="scatter",
    )(block_count, route_index, row_grads, lines, router_score.reshape(1, toks))
    return input_grad, score_grad.reshape(toks)


def solution(mesh):
    placed = (
        P("seq", "tensor"),
        P("seq", "tensor"),
        P("seq"),
        P("seq", None),
        P("seq"),
        P("seq", "tensor"),
        P("tensor", "seq"),
    )
    return jax.shard_map(
        functools.partial(per_device, mesh.shape["seq"], mesh.shape["tensor"]),
        mesh=mesh,
        in_specs=placed,
        out_specs=(P("seq", "tensor"), P("seq")),
        check_vma=False,
    )
```

time: 309 us -> 170 us (0.55)
  the two profiles are of different devices: /device:TPU:0 before, /device:TPU:25 now
where the time goes in v1:
time: 170 us; the launch traced here: 169 us
  Pallas kernels  166 us (98%)
  local copies, waits for them, and re-layouts  1.76 us (1%)
    pallas_call x1, Pallas kernels, per_device(): pl.pallas_call(functools.partial(heavy_kernel, n, nt), out_shape=(jax.Sha...  160 us
    pallas_call x1, Pallas kernels, per_device(): pl.pallas_call(scatter_kernel, grid=(toks // tile,), out_shape=(jax.Shape...  6.46 us

profile of v1, /device:TPU:25, one launch (start us, length us, event | category | flops | bytes accessed | tf_op | source)
XLA Modules:
  0.0 169.4 jit_solution(8257657639013396147)
XLA Ops:
  1.3 0.0 copy-start.1
  1.3 0.0 copy-start.3
  1.3 159.8 %heavy.1 = (bf16[512,512]{1,0:T(8,128)(2,1)}, f32[8,512]{1,0:T(8,128)}) custom-call(s32[1,512]{1,0:T(1,128)} %idx_ref.3, bf16[4096,512]{1,0:T(8,128)(2,1)} %inputs_ref.1, bf16[4096,512]{1,0:T(8,128)(2,1)} %grads_ref.1, bf16[256,2048]{1,0:T(8,128)(2,1)} %win_ref.1, bf16[2048,256]{1,0:T(8,128)(2,1)} %wout_ref.1), custom_call_target="tpu_custom_call" | custom-call | tf_op jit(solution)/shard_map/heavy/pallas_call | solution.py:380
  161.2 0.0 copy-done.1
  161.2 0.0 copy-done.3
  161.2 0.0 copy-start
  161.2 1.0 copy-done
  162.2 0.0 copy-start.2
  162.2 0.7 copy-done.2
  162.9 6.5 %scatter.1 = (bf16[4096,512]{1,0:T(8,128)(2,1)}, f32[1,4096]{1,0:T(1,128)}) custom-call(s32[1]{0:T(128)S(6)} %copy.9.count_ref, s32[1,512]{1,0:T(1,128)S(1)} %copy-done.3, bf16[512,512]{1,0:T(8,128)(2,1)S(1)} %copy-done, f32[8,512]{1,0:T(8,128)S(1)} %copy-done.2, f32[1,4096]{1,0:T(1,128)S(1)} %bitcast.2), custom_call_target="tpu_custom_call" | custom-call | tf_op jit(solution)/shard_map/scatter/pallas_call | solution.py:420
Async XLA Ops:
  1.3 159.9 %copy-start.1 = (f32[4096]{0:T(1024)S(1)}, f32[4096]{0:T(1024)}, u32[]{:S(2)}) copy-start(f32[4096]{0:T(1024)} %param.9) | copy-start | bytes 49156
  1.3 159.9 %copy-start.3 = (s32[1,512]{1,0:T(1,128)S(1)}, s32[1,512]{1,0:T(1,128)}, u32[]{:S(2)}) copy-start(s32[1,512]{1,0:T(1,128)} %idx_ref.3) | copy-start | bytes 6148
  161.2 1.0 copy-start
  162.2 0.7 copy-start.2

commit v2 on v1

--- a/solution.py
+++ b/solution.py
@@ -34,7 +34,7 @@
 def heavy_kernel(
     n, nt, idx_ref, inputs_ref, grads_ref, win_ref, wout_ref, rows_ref, score_ref,
     tok_buf, x_buf, g_buf, win_buf, wout_buf, act_buf, slope_buf, hg_buf,
-    pair_send, pair_recv, z_send, z_recv, own_buf, sc_out, sc_pair, sc_z,
+    pair_send, pair_recv, z_send, z_recv, own_buf, keep, sc_out, sc_pair, sc_z,
     tok_sem, wl_sem, w_send, w_recv, z_ssem, z_rsem, p_ssem, p_rsem,
     os_sem, or_sem, oz_ssem, oz_rsem, ss_sem, sr_sem,
 ):
@@ -59,9 +59,6 @@
     def t_out(r):
         return lax.rem(t + r, nt)
 
-    def t_in(r):
-        return lax.rem(t + nt - r, nt)
-
     load = [
         pltpu.make_async_copy(src, tok_buf.at[i], tok_sem.at[i])
         for i, src in enumerate((inputs_ref, grads_ref))
@@ -185,55 +182,91 @@
         lax.fori_loop(0, toks // step, body, 0)
         dst[...] = x_own[...].astype(BF16)
 
-    def z_copy(v, r):
-        return pltpu.make_async_remote_copy(
-            src_ref=piece(v, k, t), dst_ref=piece(v, k, t),
-            send_sem=z_ssem.at[v, r], recv_sem=z_rsem.at[v, r],
-            device_id={"tensor": t_out(r)}, device_id_type=MESH,
-        )
-
-    def z_landed(v, r):
-        return pltpu.make_async_remote_copy(
-            src_ref=piece(v, k, t_in(r)), dst_ref=piece(v, k, t_in(r)),
-            send_sem=z_ssem.at[v, r], recv_sem=z_rsem.at[v, r],
-            device_id={"tensor": t_in(r)}, device_id_type=MESH,
-        )
-
-    def pair_copy(v, r, shard):
-        return pltpu.make_async_remote_copy(
-            src_ref=piece(v, shard, t_in(r)), dst_ref=piece(v, shard, t_in(r)),
-            send_sem=p_ssem.at[v, r], recv_sem=p_rsem.at[v, r],
+    def origin(way, d):
+        return lax.rem(t + nt - d, nt) if way == 0 else lax.rem(t + d, nt)
+
+    def has(way, d):
+        return t >= d if way == 0 else t + d < nt
+
+    def z_to(way):
+        return lax.rem(t + 1, nt) if way == 0 else lax.rem(t + nt - 1, nt)
+
+    def z_copy(v, way, d):
+        ref = piece(v, k, origin(way, d))
+        return pltpu.make_async_remote_copy(
+            src_ref=ref, dst_ref=ref,
+            send_sem=z_ssem.at[v, way, d], recv_sem=z_rsem.at[v, way, d + 1],
+            device_id={"tensor": z_to(way)}, device_id_type=MESH,
+        )
+
+    def z_landed(v, way, d):
+        ref = piece(v, k, origin(way, d))
+        return pltpu.make_async_remote_copy(
+            src_ref=ref, dst_ref=ref,
+            send_sem=z_ssem.at[v, way, d], recv_sem=z_rsem.at[v, way, d],
+            device_id={"tensor": z_to(1 - way)}, device_id_type=MESH,
+        )
+
+    def pair_copy(v, way, d, shard):
+        ref = piece(v, shard, origin(way, d))
+        return pltpu.make_async_remote_copy(
+            src_ref=ref, dst_ref=ref,
+            send_sem=p_ssem.at[v, way, d], recv_sem=p_rsem.at[v, way, d],
             device_id={"seq": partner}, device_id_type=MESH,
         )
 
     def start_tokens(v):
-        for r in range(1, nt):
-            z_copy(v, r).start()
-        pair_copy(v, 0, k).start()
-
-    def pass_tokens(v):
-        for r in range(1, nt):
-            z_landed(v, r).wait_recv()
-            pair_copy(v, r, k).start()
+        for way in range(2):
+            @pl.when(has(1 - way, 1))
+            def _():
+                z_copy(v, way, 0).start()
+        pair_copy(v, 0, 0, k).start()
+
+    def pass_tokens(v, d):
+        for way in range(2):
+            @pl.when(has(way, d))
+            def _():
+                z_landed(v, way, d).wait_recv()
+                if d < nt - 1:
+                    @pl.when(has(1 - way, 1))
+                    def _():
+                        z_copy(v, way, d).start()
+                pair_copy(v, way, d, k).start()
 
     def finish_tokens(v):
-        for r in range(nt):
-            pair_copy(v, r, other).wait_recv()
+        pair_copy(v, 0, 0, other).wait_recv()
+        for way in range(2):
+            for d in range(1, nt):
+                @pl.when(has(way, d))
+                def _():
+                    pair_copy(v, way, d, other).wait_recv()
 
     def drain_tokens(v):
-        for r in range(1, nt):
-            z_copy(v, r).wait_send()
-        for r in range(nt):
-            pair_copy(v, r, k).wait_send()
+        pair_copy(v, 0, 0, k).wait_send()
+        for way in range(2):
+            for d in range(nt - 1):
+                @pl.when(has(way, d) & has(1 - way, 1))
+                def _():
+                    z_copy(v, way, d).wait_send()
+            for d in range(1, nt):
+                @pl.when(has(way, d))
+                def _():
+                    pair_copy(v, way, d, k).wait_send()
 
     start_weights(0)
     gather(0)
     start_tokens(0)
     gather(1)
+    start_tokens(1)
+    pass_tokens(0, 1)
     pass_weights(0)
     start_weights(1)
-    pass_tokens(0)
-    start_tokens(1)
+    for d in range(2, nt):
+        if d < nt - 1:
+            pass_tokens(0, d)
+        pass_tokens(1, d - 1)
+    pass_weights(1)
+    pass_tokens(0, nt - 1)
     finish_weights(0)
     finish_tokens(0)
 
@@ -250,8 +283,7 @@
 
     lax.fori_loop(0, 2 * (half // ft), hidden_step, 0)
 
-    pass_weights(1)
-    pass_tokens(1)
+    pass_tokens(1, nt - 1)
     finish_weights(1)
     finish_tokens(1)
 
@@ -285,12 +317,16 @@
             device_id={"seq": partner}, device_id_type=MESH,
         )
 
-    def o_z(r):
-        return pltpu.make_async_remote_copy(
-            src_ref=z_send.at[r - 1], dst_ref=z_recv.at[r - 1],
-            send_sem=oz_ssem.at[r], recv_sem=oz_rsem.at[r],
-            device_id={"tensor": t_out(r)}, device_id_type=MESH,
-        )
+    def o_z(p, way):
+        return pltpu.make_async_remote_copy(
+            src_ref=z_send.at[p], dst_ref=z_recv.at[way, p],
+            send_sem=oz_ssem.at[p], recv_sem=oz_rsem.at[way, p],
+            device_id={"tensor": z_to(way)}, device_id_type=MESH,
+        )
+
+    def send_sum(p, way, total):
+        z_send[p] = total.astype(BF16)
+        o_z(p, way).start()
 
     def s_pair():
         return pltpu.make_async_remote_copy(
@@ -306,47 +342,71 @@
             device_id={"tensor": t_out(r)}, device_id_type=MESH,
         )
 
-    order = list(range(1, nt)) + [0]
+    order = []
+    for i in range((nt + 1) // 2):
+        order += [nt - 1 - i] if nt - 1 - i == i else [nt - 1 - i, i]
+
     sc_pair[0] = upstream(other)
     s_pair().start()
-    for r in order:
-        pair_send[r] = grads_of(t_out(r)).astype(BF16)
-        o_pair(r).start()
+    for p in order:
+        pair_send[p] = grads_of(p).astype(BF16)
+        o_pair(p).start()
 
     mine = upstream(k)
     s_pair().wait_recv()
     sc_z[0] = mine + sc_pair[1]
     for r in range(1, nt):
         s_z(r).start()
-    for r in order:
-        part = grads_of(t_out(r))
-        o_pair(r).wait_recv()
-        part = part + pair_recv[r].astype(F32)
-        if r == 0:
-            own_buf[...] = part
-        else:
-            z_send[r - 1] = part.astype(BF16)
-            o_z(r).start()
+    for p in order:
+        keep[p] = grads_of(p)
+        o_pair(p).wait_recv()
+        keep[p] += pair_recv[p].astype(F32)
+        if p > 0:
+            @pl.when(t == 0)
+            def _():
+                send_sum(p, 0, keep[p])
+        if p < nt - 1:
+            @pl.when(t == nt - 1)
+            def _():
+                send_sum(p, 1, keep[p])
+    for p in order:
+        @pl.when((t > 0) & (t < p))
+        def _():
+            o_z(p, 0).wait_recv()
+            send_sum(p, 0, keep[p] + z_recv[0, p].astype(F32))
+
+        @pl.when((t < nt - 1) & (t > p))
+        def _():
+            o_z(p, 1).wait_recv()
+            send_sum(p, 1, keep[p] + z_recv[1, p].astype(F32))
 
     drain_weights(0)
     drain_weights(1)
     drain_tokens(0)
     drain_tokens(1)
     s_pair().wait_send()
-    for r in range(nt):
-        o_pair(r).wait_send()
+    for p in range(nt):
+        o_pair(p).wait_send()
     for r in range(1, nt):
         s_z(r).wait()
     total = sc_z[0]
     for r in range(1, nt):
         total = total + sc_z[r]
     score_ref[...] = total
-    for r in range(1, nt):
-        o_z(r).wait()
-    full = own_buf[...]
-    for r in range(1, nt):
-        full = full + z_recv[r - 1].astype(F32)
-    rows_ref[...] = full.astype(BF16)
+    for p in range(nt):
+        @pl.when(t == p)
+        def _():
+            if p > 0:
+                o_z(p, 0).wait_recv()
+                keep[p] += z_recv[0, p].astype(F32)
+            if p < nt - 1:
+                o_z(p, 1).wait_recv()
+                keep[p] += z_recv[1, p].astype(F32)
+            rows_ref[...] = keep[p].astype(BF16)
+
+        @pl.when(t != p)
+        def _():
+            o_z(p, 0).wait_send()
 
 
 def scatter_kernel(count_ref, idx_ref, rows_ref, line_ref, score_ref, grad_ref, out_ref):
@@ -396,18 +456,19 @@
             pltpu.VMEM((rows, half), BF16),
             pltpu.VMEM((nt, rows, width), BF16),
             pltpu.VMEM((nt, rows, width), BF16),
-            pltpu.VMEM((nt - 1, rows, width), BF16),
-            pltpu.VMEM((nt - 1, rows, width), BF16),
+            pltpu.VMEM((nt, rows, width), BF16),
+            pltpu.VMEM((2, nt, rows, width), BF16),
             pltpu.VMEM((rows, width), F32),
+            pltpu.VMEM((nt, rows, width), F32),
             pltpu.VMEM((rows, 128), F32),
             pltpu.VMEM((2, 8, rows), F32),
             pltpu.VMEM((nt, 8, rows), F32),
             dma((2,)), dma((2,)),
             dma((2, chips, 2)), dma((2, chips, 2)),
-            dma((2, nt)), dma((2, nt)),
-            dma((2, nt)), dma((2, nt)),
+            dma((2, 2, nt)), dma((2, 2, nt)),
+            dma((2, 2, nt)), dma((2, 2, nt)),
             dma((nt,)), dma((nt,)),
-            dma((nt,)), dma((nt,)),
+            dma((nt,)), dma((2, nt)),
             dma((nt,)), dma((nt,)),
         ],
         compiler_params=pltpu.CompilerParams(

time: 170 us -> 155 us (0.912)
  the two profiles are of different devices: /device:TPU:25 before, /device:TPU:0 now
where the time goes in v2:
time: 155 us
  Pallas kernels  152 us (98%)
  local copies, waits for them, and re-layouts  1.76 us (1%)
    pallas_call x1, Pallas kernels, per_device(): pl.pallas_call(functools.partial(heavy_kernel, n, nt), out_shape=(jax.Sha...  146 us
    pallas_call x1, Pallas kernels, per_device(): pl.pallas_call(scatter_kernel, grid=(toks // tile,), out_shape=(jax.Shape...  6.46 us

profile of v2, /device:TPU:0, one launch (start us, length us, event | category | flops | bytes accessed | tf_op | source)
XLA Modules:
  0.0 155.1 jit_solution(3828550337509897493)
XLA Ops:
  1.3 0.0 copy-start.1
  1.3 0.0 copy-start.3
  1.3 145.6 %heavy.1 = (bf16[512,512]{1,0:T(8,128)(2,1)}, f32[8,512]{1,0:T(8,128)}) custom-call(s32[1,512]{1,0:T(1,128)} %idx_ref.3, bf16[4096,512]{1,0:T(8,128)(2,1)} %inputs_ref.1, bf16[4096,512]{1,0:T(8,128)(2,1)} %grads_ref.1, bf16[256,2048]{1,0:T(8,128)(2,1)} %win_ref.1, bf16[2048,256]{1,0:T(8,128)(2,1)} %wout_ref.1), custom_call_target="tpu_custom_call" | custom-call | tf_op jit(solution)/shard_map/heavy/pallas_call | solution.py:440
  146.9 0.0 copy-done.1
  146.9 0.0 copy-done.3
  146.9 0.0 copy-start
  146.9 1.0 copy-done
  147.9 0.0 copy-start.2
  148.0 0.7 copy-done.2
  148.7 6.5 %scatter.1 = (bf16[4096,512]{1,0:T(8,128)(2,1)}, f32[1,4096]{1,0:T(1,128)}) custom-call(s32[1]{0:T(128)S(6)} %copy.9.count_ref, s32[1,512]{1,0:T(1,128)S(1)} %copy-done.3, bf16[512,512]{1,0:T(8,128)(2,1)S(1)} %copy-done, f32[8,512]{1,0:T(8,128)S(1)} %copy-done.2, f32[1,4096]{1,0:T(1,128)S(1)} %bitcast.2), custom_call_target="tpu_custom_call" | custom-call | tf_op jit(solution)/shard_map/scatter/pallas_call | solution.py:481
Async XLA Ops:
  1.3 145.6 %copy-start.1 = (f32[4096]{0:T(1024)S(1)}, f32[4096]{0:T(1024)}, u32[]{:S(2)}) copy-start(f32[4096]{0:T(1024)} %param.9) | copy-start | bytes 49156
  1.3 145.6 %copy-start.3 = (s32[1,512]{1,0:T(1,128)S(1)}, s32[1,512]{1,0:T(1,128)}, u32[]{:S(2)}) copy-start(s32[1,512]{1,0:T(1,128)} %idx_ref.3) | copy-start | bytes 6148
  146.9 1.0 copy-start
  147.9 0.7 copy-start.2

commit v3 on v2

--- a/solution.py
+++ b/solution.py
@@ -34,7 +34,7 @@
 def heavy_kernel(
     n, nt, idx_ref, inputs_ref, grads_ref, win_ref, wout_ref, rows_ref, score_ref,
     tok_buf, x_buf, g_buf, win_buf, wout_buf, act_buf, slope_buf, hg_buf,
-    pair_send, pair_recv, z_send, z_recv, own_buf, keep, sc_out, sc_pair, sc_z,
+    pair_send, pair_recv, z_send, z_recv, own_buf, keep, sc_out, sc_own, sc_pair, sc_z,
     tok_sem, wl_sem, w_send, w_recv, z_ssem, z_rsem, p_ssem, p_rsem,
     os_sem, or_sem, oz_ssem, oz_rsem, ss_sem, sr_sem,
 ):
@@ -287,15 +287,23 @@
     finish_weights(1)
     finish_tokens(1)
 
-    def upstream(shard):
+    hr = rows // 2
+    own_rows = pl.ds(pl.multiple_of(k * hr, hr), hr)
+    other_rows = pl.ds(pl.multiple_of(other * hr, hr), hr)
+
+    def upstream(h):
+        span = pl.ds(h * hr, hr)
         sc_out[...] = jnp.zeros_like(sc_out)
+
+        def both(ref, cols):
+            return jnp.concatenate([ref[0, span, cols], ref[1, span, cols]], axis=0)
 
         def step(f, carry):
             cols = pl.ds(pl.multiple_of(f * ft, ft), ft)
             weights = jnp.concatenate([wout_buf[i, cols, :] for i in range(n)], axis=1)
-            up = dot(g_buf[shard], weights, NT)
-            hg_buf[:, cols] = (up * slope_buf[shard, :, cols]).astype(BF16)
-            terms = up * act_buf[shard, :, cols].astype(F32)
+            up = dot(both(g_buf, slice(None)), weights, NT)
+            hg_buf[:, cols] = (up * both(slope_buf, cols)).astype(BF16)
+            terms = up * both(act_buf, cols).astype(F32)
             part = terms[:, :128]
             for i in range(1, ft // 128):
                 part = part + terms[:, i * 128:(i + 1) * 128]
@@ -304,29 +312,36 @@
 
         lax.fori_loop(0, half // ft, step, 0)
         line = jnp.sum(jnp.transpose(sc_out[...]), axis=0, keepdims=True)
-        return jnp.broadcast_to(line, (8, rows))
+        for shard in range(2):
+            sc_own[shard, :, span] = jnp.broadcast_to(line[:, shard * hr:(shard + 1) * hr], (8, hr))
 
     def grads_of(column):
-        span = pl.ds(pl.multiple_of(column * width, width), width)
+        span = pl.ds(column * width, width)
         return dot(hg_buf[...], win_buf[span, :], NT)
 
-    def o_pair(r):
-        return pltpu.make_async_remote_copy(
-            src_ref=pair_send.at[r], dst_ref=pair_recv.at[r],
-            send_sem=os_sem.at[r], recv_sem=or_sem.at[r],
+    def o_pair(h, p):
+        span = pl.ds(h * hr, hr)
+        return pltpu.make_async_remote_copy(
+            src_ref=pair_send.at[p, span, :], dst_ref=pair_recv.at[p, span, :],
+            send_sem=os_sem.at[h, p], recv_sem=or_sem.at[h, p],
             device_id={"seq": partner}, device_id_type=MESH,
         )
 
-    def o_z(p, way):
-        return pltpu.make_async_remote_copy(
-            src_ref=z_send.at[p], dst_ref=z_recv.at[way, p],
-            send_sem=oz_ssem.at[p], recv_sem=oz_rsem.at[way, p],
+    def o_z(h, p, way):
+        span = pl.ds(h * hr, hr)
+        return pltpu.make_async_remote_copy(
+            src_ref=z_send.at[p, span, :], dst_ref=z_recv.at[way, p, span, :],
+            send_sem=oz_ssem.at[h, p], recv_sem=oz_rsem.at[h, way, p],
             device_id={"tensor": z_to(way)}, device_id_type=MESH,
         )
 
-    def send_sum(p, way, total):
-        z_send[p] = total.astype(BF16)
-        o_z(p, way).start()
+    def arrived(h, p, way):
+        o_z(h, p, way).wait_recv()
+        return z_recv[way, p, h * hr:(h + 1) * hr, :].astype(F32)
+
+    def send_sum(h, p, way, total):
+        z_send[p, h * hr:(h + 1) * hr, :] = total.astype(BF16)
+        o_z(h, p, way).start()
 
     def s_pair():
         return pltpu.make_async_remote_copy(
@@ -346,67 +361,80 @@
     for i in range((nt + 1) // 2):
         order += [nt - 1 - i] if nt - 1 - i == i else [nt - 1 - i, i]
 
-    sc_pair[0] = upstream(other)
+    def make(h, p):
+        keep[h, p] = grads_of(p)
+        pair_send[p, h * hr:(h + 1) * hr, :] = keep[h, p, other_rows, :].astype(BF16)
+        o_pair(h, p).start()
+
+    def add_pair(h, p):
+        o_pair(h, p).wait_recv()
+        keep[h, p, own_rows, :] += pair_recv[p, h * hr:(h + 1) * hr, :].astype(F32)
+        if p > 0:
+            @pl.when(t == 0)
+            def _():
+                send_sum(h, p, 0, keep[h, p, own_rows, :])
+        if p < nt - 1:
+            @pl.when(t == nt - 1)
+            def _():
+                send_sum(h, p, 1, keep[h, p, own_rows, :])
+
+    def hop(h, p):
+        @pl.when((t > 0) & (t < p))
+        def _():
+            send_sum(h, p, 0, keep[h, p, own_rows, :] + arrived(h, p, 0))
+
+        @pl.when((t < nt - 1) & (t > p))
+        def _():
+            send_sum(h, p, 1, keep[h, p, own_rows, :] + arrived(h, p, 1))
+
+    for h in range(2):
+        upstream(h)
+        if h == 1:
+            for p in order[:2]:
+                hop(0, p)
+        make(h, order[0])
+        for before, p in zip(order, order[1:]):
+            make(h, p)
+            add_pair(h, before)
+        add_pair(h, order[-1])
+
+    sc_pair[0] = sc_own[other]
     s_pair().start()
-    for p in order:
-        pair_send[p] = grads_of(p).astype(BF16)
-        o_pair(p).start()
-
-    mine = upstream(k)
+    for p in order[2:]:
+        hop(0, p)
     s_pair().wait_recv()
-    sc_z[0] = mine + sc_pair[1]
+    sc_z[0] = sc_own[k] + sc_pair[1]
     for r in range(1, nt):
         s_z(r).start()
     for p in order:
-        keep[p] = grads_of(p)
-        o_pair(p).wait_recv()
-        keep[p] += pair_recv[p].astype(F32)
-        if p > 0:
-            @pl.when(t == 0)
-            def _():
-                send_sum(p, 0, keep[p])
-        if p < nt - 1:
-            @pl.when(t == nt - 1)
-            def _():
-                send_sum(p, 1, keep[p])
-    for p in order:
-        @pl.when((t > 0) & (t < p))
-        def _():
-            o_z(p, 0).wait_recv()
-            send_sum(p, 0, keep[p] + z_recv[0, p].astype(F32))
-
-        @pl.when((t < nt - 1) & (t > p))
-        def _():
-            o_z(p, 1).wait_recv()
-            send_sum(p, 1, keep[p] + z_recv[1, p].astype(F32))
+        hop(1, p)
 
     drain_weights(0)
     drain_weights(1)
     drain_tokens(0)
     drain_tokens(1)
     s_pair().wait_send()
-    for p in range(nt):
-        o_pair(p).wait_send()
     for r in range(1, nt):
         s_z(r).wait()
     total = sc_z[0]
     for r in range(1, nt):
         total = total + sc_z[r]
     score_ref[...] = total
-    for p in range(nt):
-        @pl.when(t == p)
-        def _():
-            if p > 0:
-                o_z(p, 0).wait_recv()
-                keep[p] += z_recv[0, p].astype(F32)
-            if p < nt - 1:
-                o_z(p, 1).wait_recv()
-                keep[p] += z_recv[1, p].astype(F32)
-            rows_ref[...] = keep[p].astype(BF16)
-
-        @pl.when(t != p)
-        def _():
-            o_z(p, 0).wait_send()
+    for h in range(2):
+        for p in range(nt):
+            o_pair(h, p).wait_send()
+
+            @pl.when(t == p)
+            def _():
+                if p > 0:
+                    keep[h, p, own_rows, :] += arrived(h, p, 0)
+                if p < nt - 1:
+                    keep[h, p, own_rows, :] += arrived(h, p, 1)
+                rows_ref[h * hr:(h + 1) * hr, :] = keep[h, p, own_rows, :].astype(BF16)
+
+            @pl.when(t != p)
+            def _():
+                o_z(h, p, 0).wait_send()
 
 
 def scatter_kernel(count_ref, idx_ref, rows_ref, line_ref, score_ref, grad_ref, out_ref):
@@ -459,16 +487,17 @@
             pltpu.VMEM((nt, rows, width), BF16),
             pltpu.VMEM((2, nt, rows, width), BF16),
             pltpu.VMEM((rows, width), F32),
-            pltpu.VMEM((nt, rows, width), F32),
+            pltpu.VMEM((2, nt, rows, width), F32),
             pltpu.VMEM((rows, 128), F32),
+            pltpu.VMEM((2, 8, rows), F32),
             pltpu.VMEM((2, 8, rows), F32),
             pltpu.VMEM((nt, 8, rows), F32),
             dma((2,)), dma((2,)),
             dma((2, chips, 2)), dma((2, chips, 2)),
             dma((2, 2, nt)), dma((2, 2, nt)),
             dma((2, 2, nt)), dma((2, 2, nt)),
-            dma((nt,)), dma((nt,)),
-            dma((nt,)), dma((2, nt)),
+            dma((2, nt)), dma((2, nt)),
+            dma((2, nt)), dma((2, 2, nt)),
             dma((nt,)), dma((nt,)),
         ],
         compiler_params=pltpu.CompilerParams(

time: 155 us -> 153 us (0.987)
  Pallas kernels: 152 us -> 150 us
    pallas_call x1, Pallas kernels: 146 us -> 144 us  [per_device(): pl.pallas_call(functools.partial(heavy_kernel, n, nt), out_shape=(jax.Sha...]
where the time goes in v3:
time: 153 us
  Pallas kernels  150 us (98%)
  local copies, waits for them, and re-layouts  1.76 us (1%)
    pallas_call x1, Pallas kernels, per_device(): pl.pallas_call(functools.partial(heavy_kernel, n, nt), out_shape=(jax.Sha...  144 us
    pallas_call x1, Pallas kernels, per_device(): pl.pallas_call(scatter_kernel, grid=(toks // tile,), out_shape=(jax.Shape...  6.46 us

profile of v3, /device:TPU:0, one launch (start us, length us, event | category | flops | bytes accessed | tf_op | source)
XLA Modules:
  0.0 153.1 jit_solution(3281958640666042459)
XLA Ops:
  1.3 0.0 copy-start.1
  1.3 0.0 copy-start.3
  1.3 143.6 %heavy.1 = (bf16[512,512]{1,0:T(8,128)(2,1)}, f32[8,512]{1,0:T(8,128)}) custom-call(s32[1,512]{1,0:T(1,128)} %idx_ref.3, bf16[4096,512]{1,0:T(8,128)(2,1)} %inputs_ref.1, bf16[4096,512]{1,0:T(8,128)(2,1)} %grads_ref.1, bf16[256,2048]{1,0:T(8,128)(2,1)} %win_ref.1, bf16[2048,256]{1,0:T(8,128)(2,1)} %wout_ref.1), custom_call_target="tpu_custom_call" | custom-call | tf_op jit(solution)/shard_map/heavy/pallas_call | solution.py:468
  144.9 0.0 copy-done.1
  144.9 0.0 copy-done.3
  144.9 0.0 copy-start
  144.9 1.0 copy-done
  146.0 0.0 copy-start.2
  146.0 0.7 copy-done.2
  146.7 6.5 %scatter.1 = (bf16[4096,512]{1,0:T(8,128)(2,1)}, f32[1,4096]{1,0:T(1,128)}) custom-call(s32[1]{0:T(128)S(6)} %copy.9.count_ref, s32[1,512]{1,0:T(1,128)S(1)} %copy-done.3, bf16[512,512]{1,0:T(8,128)(2,1)S(1)} %copy-done, f32[8,512]{1,0:T(8,128)S(1)} %copy-done.2, f32[1,4096]{1,0:T(1,128)S(1)} %bitcast.2), custom_call_target="tpu_custom_call" | custom-call | tf_op jit(solution)/shard_map/scatter/pallas_call | solution.py:510
Async XLA Ops:
  1.3 143.6 %copy-start.1 = (f32[4096]{0:T(1024)S(1)}, f32[4096]{0:T(1024)}, u32[]{:S(2)}) copy-start(f32[4096]{0:T(1024)} %param.9) | copy-start | bytes 49156
  1.3 143.6 %copy-start.3 = (s32[1,512]{1,0:T(1,128)S(1)}, s32[1,512]{1,0:T(1,128)}, u32[]{:S(2)}) copy-start(s32[1,512]{1,0:T(1,128)} %idx_ref.3) | copy-start | bytes 6148
  144.9 1.0 copy-start
  146.0 0.7 copy-start.2
